TPU v7x, 512 devices: a whole 4x4x16 slice. The times are simulated.
512 devices in a mesh: wide: 128 (over z_lo, x, y, core), narrow: 4 (over z_hi).
Axes of the slice: x: 4, y: 4, z: 16 (z_hi: 4, z_lo: 4; z = z_hi * 4 + z_lo), core: 2. Of those that a mesh axis runs over, the one named last changes fastest.
Arguments:
- grad_in: float32 [131072, 128], P(('wide', 'narrow')), may hold values from -6 to 6
- phi_slope: bfloat16 [131072, 128], P(('wide', 'narrow')), may hold values from 0.049804688 to 1
- activations: bfloat16 [131072, 128], P(('wide', 'narrow')), may hold values from -6 to 6
- weight: bfloat16 [128, 128], replicated, may hold values from -0.5 to 0.5
- local_tiles: bfloat16 [512, 8, 128, 128], P(('wide', 'narrow')), may hold values from -0.0625 to 0.0625
- local_rows: int32 [512, 8], P(('wide', 'narrow')), may hold values from 0 to 1, as said below
- local_cols: int32 [512, 8], P(('wide', 'narrow')), may hold values from 0 to 7, as said below
- local_count: int32 [512], P(('wide', 'narrow')), may hold values from 1 to 8, 3072 in all
- remote_tiles: bfloat16 [512, 112, 128, 128], P(('wide', 'narrow')), may hold values from -0.0625 to 0.0625
- remote_rows: int32 [512, 112], P(('wide', 'narrow')), may hold values from 0 to 1, as said below
- remote_cols: int32 [512, 112], P(('wide', 'narrow')), may hold values from 0 to 55, as said below
- remote_count: int32 [512], P(('wide', 'narrow')), may hold values from 1 to 112, 43008 in all
- send_list: int32 [512, 128, 56], P(('wide', 'narrow')), may hold values from 0 to 1023
Outputs:
- adjoint: float32 [131072, 128], P(('wide', 'narrow'))
- weight_grad: float32 [128, 128], replicated
Inputs may be any that keep to these rules, and one draw needn't show every extreme that they name: `local_count`: each device's live local tile slots; slots from this count onward are ignored, and some device uses all 8. `remote_count`: each device's live remote tile slots; slots from this count onward are ignored, and some device uses all 112. On one device no two local slots have the same pair of local_rows and local_cols. `local_cols`: see local_rows. On one device no two remote slots have the same pair of remote_rows and remote_cols. `remote_cols`: see remote_rows.
All inputs are finite; a program needn't handle non-finite values.
Results may differ from a plain program's by a relative error of at most 0.0031.
Values may be sent and summed in bfloat16 or wider, within the bound.
A program may use at most 64 MiB of HBM per device.

v0:
```python
import jax
import jax.numpy as jnp
from jax import lax
from jax.sharding import PartitionSpec as P

ITERS = 2
GAMMA = 0.5


def row_table(row_ids, live_count, blocks):
    slot_count = row_ids.shape[0]
    is_live = jnp.arange(slot_count, dtype=jnp.int32) < live_count
    matches = row_ids[None, :] == jnp.arange(blocks, dtype=jnp.int32)[:, None]
    return (matches & is_live[None, :]).astype(jnp.float32)


def tile_product(tile_values, table, picked, hidden):
    product = jnp.einsum("kij,kjh->kih", tile_values, picked, preferred_element_type=jnp.float32)
    summed = jnp.einsum("rk,kih->rih", table, product, precision=lax.Precision.HIGHEST)
    return summed.reshape(-1, hidden)


def per_device(
    grad_in,
    phi_slope,
    activations,
    weight,
    local_tiles,
    local_rows,
    local_cols,
    local_count,
    remote_tiles,
    remote_rows,
    remote_cols,
    remote_count,
    send_list,
):
    dev_rows = grad_in.shape[0]
    hidden = grad_in.shape[1]
    tile_size = local_tiles.shape[2]
    blocks = dev_rows // tile_size
    group_blocks = lax.axis_size("narrow") * blocks
    near_table = row_table(local_rows[0], local_count[0], blocks)
    far_table = row_table(remote_rows[0], remote_count[0], blocks)
    all_tiles = jnp.concatenate([local_tiles[0], remote_tiles[0]], axis=0)
    all_table = jnp.concatenate([near_table, far_table], axis=1)
    all_cols = jnp.concatenate([local_cols[0], remote_cols[0] + group_blocks], axis=0)
    adjoint = grad_in
    for iteration in range(ITERS):
        mapped = jnp.einsum(
            "nk,hk->nh", adjoint.astype(jnp.bfloat16), weight, preferred_element_type=jnp.float32
        )
        message = (mapped * phi_slope).astype(jnp.bfloat16)
        gathered = lax.all_gather(message, "narrow", axis=0, tiled=True)
        outgoing = gathered[send_list[0]]
        incoming = lax.all_to_all(outgoing, "wide", split_axis=0, concat_axis=0, tiled=True)
        halo_blocks = incoming.reshape(-1, tile_size, hidden)
        own_blocks = gathered.reshape(-1, tile_size, hidden)
        sources = jnp.concatenate([own_blocks, halo_blocks], axis=0)
        spread = tile_product(all_tiles, all_table, sources[all_cols], hidden)
        adjoint = grad_in + GAMMA * spread
    partial_sum = lax.dot_general(
        activations,
        adjoint.astype(jnp.bfloat16),
        (((0,), (0,)), ((), ())),
        preferred_element_type=jnp.float32,
    )
    summed = lax.psum(partial_sum, ("wide", "narrow"))
    node_total = dev_rows * lax.axis_size("wide") * lax.axis_size("narrow")
    weight_grad = summed * (GAMMA / jnp.sqrt(jnp.float32(node_total)))
    return (adjoint, weight_grad)


def solution(mesh):
    placed = (
        P(("wide", "narrow"), None),
        P(("wide", "narrow"), None),
        P(("wide", "narrow"), None),
        P(),
        P(("wide", "narrow"), None, None, None),
        P(("wide", "narrow"), None),
        P(("wide", "narrow"), None),
        P(("wide", "narrow")),
        P(("wide", "narrow"), None, None, None),
        P(("wide", "narrow"), None),
        P(("wide", "narrow"), None),
        P(("wide", "narrow")),
        P(("wide", "narrow"), None, None),
    )
    return jax.shard_map(
        per_device,
        mesh=mesh,
        in_specs=placed,
        out_specs=(P(("wide", "narrow"), None), P()),
        check_vma=False,
    )
```

profile of v0, /device:TPU:1, one launch (start us, length us, event | category | flops | bytes accessed | tf_op | source)
XLA Modules:
  0.0 687.4 jit_solution(18382776733626664124)
XLA Ops:
  7.2 0.0 copy-start
  7.2 1.1 fusion.12
  8.3 25.3 %all_gather.6 = bf16[1024,128]{1,0:T(8,128)(2,1)S(1)} all-gather(bf16[256,128]{1,0:T(8,128)(2,1)S(1)} %fusion.12), channel_id=1, replica_groups=mesh['wide'=128,'narrow'=4] {'narrow'}, dimensions={0}, use_global_device_ids=true | all-gather | bytes 327680 | tf_op jit(solution)/shard_map/all_gather | solution.py:54
  33.6 0.8 compare_select_fusion
  34.3 0.1 copy.16
  34.4 0.1 reshape.145
  34.5 0.0 copy-start.7
  34.5 0.0 copy-start.8
  34.6 0.0 copy-start.9
  34.6 0.0 copy-start.10
  34.6 25.5 %gather_fusion = bf16[7168,128]{1,0:T(8,128)(2,1)} fusion(bf16[1024,128]{1,0:T(8,128)(2,1)S(1)} %all_gather.6, s32[7168]{0:T(1024)S(1)} %broadcast_clamp_fusion), kind=kCustom, calls=%fused_computation | custom fusion | bytes 3698688 | tf_op jit(solution)/shard_map/gather | solution.py:55
  60.1 13.1 %all-to-all-start = ((bf16[128,56,128]{2,1,0:T(8,128)(2,1)}), bf16[128,56,128]{2,1,0:T(8,128)(2,1)S(1)}, u32[]{:S(2)}, u32[]{:S(2)}) async-start(bf16[128,56,128]{2,1,0:T(8,128)(2,1)} %bitcast.47), calls=%async_computation | async-start | bytes 3670016 | tf_op jit(solution)/shard_map/all_to_all | solution.py:56
  73.3 0.2 all-reduce.2.cloned.1.call-start
  74.8 0.0 copy-done.7
  74.8 0.0 copy-done.8
  74.9 0.1 fusion.17
  74.9 0.0 copy-done.9
  75.0 0.0 copy-done.10
  75.0 44.7 %all-to-all-done = bf16[128,56,128]{2,1,0:T(8,128)(2,1)S(1)} async-done(((bf16[128,56,128]{2,1,0:T(8,128)(2,1)}), bf16[128,56,128]{2,1,0:T(8,128)(2,1)S(1)}, u32[]{:S(2)}, u32[]{:S(2)}) %all-to-all-start) | async-done | bytes 1835040 | tf_op jit(solution)/shard_map/all_to_all | solution.py:56
  119.7 0.0 copy-start.1
  119.7 1.3 copy-done.1
  120.9 1.7 pad_maximum_fusion.3
  122.6 0.0 copy-start.3
  122.6 2.9 gather_fusion.1
  125.6 0.0 copy-done.3
  125.6 4.4 fusion.5
  130.0 0.0 copy-start.2
  130.0 0.0 copy-start.5
  130.0 0.0 copy-start.6
  130.0 7.1 %fusion.6 = f32[2,128,128]{2,0,1:T(2,128)S(1)} fusion(f32[120,128,128]{2,1,0:T(8,128)S(1)} %fusion.5, pred[2,112]{1,0:T(4,128)(4,1)S(1)} %compare_and_fusion, pred[2,8]{1,0:T(4,128)(4,1)S(1)} %compare_and_fusion.1), kind=kOutput, calls=%fused_computation.13 | convolution fusion | flops 47218928 | bytes 7995632 | tf_op jit(solution)/shard_map/rk,kih->rih/dot_general | solution.py:19
  137.1 0.0 copy-done.2
  137.1 0.0 copy-done.5
  137.1 0.0 copy-done.6
  137.2 0.2 fusion.13
  137.3 18.3 %all_gather.7 = bf16[1024,128]{1,0:T(8,128)(2,1)S(1)} all-gather(bf16[256,128]{1,0:T(8,128)(2,1)S(1)} %fusion.13), channel_id=1, replica_groups=mesh['wide'=128,'narrow'=4] {'narrow'}, dimensions={0}, use_global_device_ids=true | all-gather | bytes 327680 | tf_op jit(solution)/shard_map/all_gather | solution.py:54
  155.6 21.1 %gather_fusion.2 = bf16[7168,128]{1,0:T(8,128)(2,1)S(1)} fusion(bf16[1024,128]{1,0:T(8,128)(2,1)S(1)} %all_gather.7, s32[7168]{0:T(1024)S(1)} %broadcast_clamp_fusion), kind=kCustom, calls=%fused_computation.2 | custom fusion | bytes 3698688 | tf_op jit(solution)/shard_map/gather | solution.py:55
  176.7 53.7 %all_to_all.10 = bf16[128,56,128]{2,1,0:T(8,128)(2,1)S(1)} all-to-all(bf16[128,56,128]{2,1,0:T(8,128)(2,1)S(1)} %bitcast.48), channel_id=1, replica_groups=mesh['wide'=128,'narrow'=4] {'wide'}, dimensions={0} | all-to-all | bytes 3670016 | tf_op jit(solution)/shard_map/all_to_all | solution.py:56
  230.3 0.2 pad_maximum_fusion.4
  230.5 2.9 gather_fusion.3
  233.4 4.4 fusion.4
  237.9 7.1 %fusion.9 = f32[2,128,128]{2,0,1:T(2,128)S(1)} fusion(f32[120,128,128]{2,1,0:T(8,128)S(1)} %fusion.4, pred[2,112]{1,0:T(4,128)(4,1)S(1)} %compare_and_fusion, pred[2,8]{1,0:T(4,128)(4,1)S(1)} %compare_and_fusion.1), kind=kOutput, calls=%fused_computation.14 | convolution fusion | flops 47218928 | bytes 7995632 | tf_op jit(solution)/shard_map/rk,kih->rih/dot_general | solution.py:19
  244.9 0.0 copy-done
  245.0 0.0 copy-start.4
  245.0 0.8 convolution_bitcast_fusion
  245.8 0.0 all-reduce.2.cloned.1.call-update
  245.8 433.1 %all-reduce.2.cloned.1.call-done = f32[128,128]{0,1:T(8,128)} async-done(((f32[128,128]{0,1:T(8,128)}), f32[128,128]{0,1:T(8,128)}) %all-reduce.2.cloned.1.call-update) | async-done | bytes 65552 | tf_op jit(solution)/shard_map/psum | solution.py:68
  679.0 0.8 broadcast_multiply_fusion
  679.8 0.7 copy.19
  680.5 0.0 copy-done.4
  (11 shorter events, 0.1 us)
Async XLA Ops:
  7.2 237.8 %copy-start = (bf16[256,128]{1,0:T(8,128)(2,1)S(1)}, bf16[256,128]{1,0:T(8,128)(2,1)}, u32[]{:S(2)}) copy-start(bf16[256,128]{1,0:T(8,128)(2,1)} %param.15) | copy-start | bytes 196612
  34.5 40.3 %copy-start.7 = (s32[1,112]{1,0:T(1,128)S(1)}, s32[1,112]{1,0:T(1,128)}, u32[]{:S(2)}) copy-start(s32[1,112]{1,0:T(1,128)} %param.23) | copy-start | bytes 1348
  34.5 40.3 %copy-start.8 = (s32[1,8]{1,0:T(1,128)S(1)}, s32[1,8]{1,0:T(1,128)}, u32[]{:S(2)}) copy-start(s32[1,8]{1,0:T(1,128)} %param.19) | copy-start | bytes 100
  34.6 40.4 %copy-start.9 = (s32[1,112]{1,0:T(1,128)S(1)}, s32[1,112]{1,0:T(1,128)}, u32[]{:S(2)}) copy-start(s32[1,112]{1,0:T(1,128)} %param.22) | copy-start | bytes 1348
  34.6 40.4 %copy-start.10 = (s32[1,8]{1,0:T(1,128)S(1)}, s32[1,8]{1,0:T(1,128)}, u32[]{:S(2)}) copy-start(s32[1,8]{1,0:T(1,128)} %param.18) | copy-start | bytes 100
  60.1 59.5 %all-to-all-start = ((bf16[128,56,128]{2,1,0:T(8,128)(2,1)}), bf16[128,56,128]{2,1,0:T(8,128)(2,1)S(1)}, u32[]{:S(2)}, u32[]{:S(2)}) async-start(bf16[128,56,128]{2,1,0:T(8,128)(2,1)} %bitcast.47), calls=%async_computation | async-start | bytes 3670016 | tf_op jit(solution)/shard_map/all_to_all | solution.py:56
  73.3 605.7 %all-reduce.2.cloned.1.call-start = ((), (), s32[]{:S(2)}) async-start(), calls=%async_computation.2 | async-start | bytes 131072 | tf_op jit(solution)/shard_map/psum | solution.py:68
  119.7 1.3 copy-start.1
  122.6 2.9 copy-start.3
  130.0 7.1 %copy-start.2 = (f32[256,128]{1,0:T(8,128)S(1)}, f32[256,128]{1,0:T(8,128)}, u32[]{:S(2)}) copy-start(f32[256,128]{1,0:T(8,128)} %param.13) | copy-start | bytes 393220
  130.0 7.1 %copy-start.5 = (bf16[256,128]{1,0:T(8,128)(2,1)S(1)}, bf16[256,128]{1,0:T(8,128)(2,1)}, u32[]{:S(2)}) copy-start(bf16[256,128]{1,0:T(8,128)(2,1)} %param.14) | copy-start | bytes 196612
  130.0 7.1 %copy-start.6 = (bf16[128,128]{1,0:T(8,128)(2,1)S(1)}, bf16[128,128]{1,0:T(8,128)(2,1)}, u32[]{:S(2)}) copy-start(bf16[128,128]{1,0:T(8,128)(2,1)} %param.16) | copy-start | bytes 98308
  245.0 435.6 %copy-start.4 = (f32[256,128]{1,0:T(8,128)}, f32[256,128]{1,0:T(8,128)S(1)}, u32[]{:S(2)}) copy-start(f32[256,128]{1,0:T(8,128)S(1)} %bitcast_add_fusion) | copy-start | bytes 393220
Sparse Core Ops, SparseCore 0:
  245.9 432.9 all-reduce.1
where the time goes:
time: 688 us; the launch traced here: 687 us
  waiting for transfers between devices  478 us (69%)
  blocking collectives  97.2 us (14%)
  local copies, waits for them, and re-layouts  54.7 us (8%)
  matrix products  25.1 us (4%)
  between operations  15.6 us (2%)
  starting transfers between devices  13.4 us (2%)
    psum x1, waiting for transfers between devices, per_device(): summed = lax.psum(partial_sum, ('wide', 'narrow'))  433 us
    all_to_all x1, blocking collectives, per_device(): lax.all_to_all(outgoing, 'wide', split_axis=0, concat_axis=0, tiled=True)  53.7 us
    gather x2, local copies, waits for them, and re-layouts, per_device(): outgoing = gathered[send_list[0]]  46.6 us
    all_to_all x1, waiting for transfers between devices, per_device(): lax.all_to_all(outgoing, 'wide', split_axis=0, concat_axis=0, tiled=True)  44.7 us
    all_gather x2, blocking collectives, per_device(): gathered = lax.all_gather(message, 'narrow', axis=0, tiled=True)  43.5 us
    dot_general x2, matrix products, tile_product(): jnp.einsum('rk,kih->rih', table, product, precision=lax.Precision.HIGHEST)  14.1 us
  transfers between devices with their start and end apart: 2, of which 2 were waited for; matrix products, arithmetic and copies ran while one was open for 0% of the time, Pallas kernels for 0%

commit v1 on v0

--- a/solution.py
+++ b/solution.py
@@ -65,7 +65,7 @@
         (((0,), (0,)), ((), ())),
         preferred_element_type=jnp.float32,
     )
-    summed = lax.psum(partial_sum, ("wide", "narrow"))
+    summed = jnp.sum(lax.all_gather(partial_sum, ("wide", "narrow")), axis=0)
     node_total = dev_rows * lax.axis_size("wide") * lax.axis_size("narrow")
     weight_grad = summed * (GAMMA / jnp.sqrt(jnp.float32(node_total)))
     return (adjoint, weight_grad)

time: 688 us -> 1460 us (2.12)
  waiting for transfers between devices: 478 us -> 1230 us
  local copies, waits for them, and re-layouts: 54.7 us -> 72.1 us
    all_gather x0 -> x1, waiting for transfers between devices: none -> 1180 us  [per_device(): summed = jnp.sum(lax.all_gather(partial_sum, ('wide', 'narrow')), axis=0)]
    psum x1 -> x0, waiting for transfers between devices: 433 us -> none  [per_device(): summed = lax.psum(partial_sum, ('wide', 'narrow'))]
    unnamed x23 -> x26, local copies, waits for them, and re-layouts: 2.06 us -> 19.3 us
where the time goes in v1:
time: 1460 us
  waiting for transfers between devices  1230 us (84%)
  blocking collectives  97 us (7%)
  local copies, waits for them, and re-layouts  72.1 us (5%)
  matrix products  25 us (2%)
  between operations  15.6 us (1%)
    all_gather x1, waiting for transfers between devices, per_device(): summed = jnp.sum(lax.all_gather(partial_sum, ('wide', 'narrow')), axis=0)  1180 us
    all_to_all x1, blocking collectives, per_device(): lax.all_to_all(outgoing, 'wide', split_axis=0, concat_axis=0, tiled=True)  53.5 us
    gather x2, local copies, waits for them, and re-layouts, per_device(): outgoing = gathered[send_list[0]]  46.8 us
    all_to_all x1, waiting for transfers between devices, per_device(): lax.all_to_all(outgoing, 'wide', split_axis=0, concat_axis=0, tiled=True)  44.7 us
    all_gather x2, blocking collectives, per_device(): gathered = lax.all_gather(message, 'narrow', axis=0, tiled=True)  43.5 us
  transfers between devices with their start and end apart: 2, of which 2 were waited for; matrix products, arithmetic and copies ran while one was open for 0% of the time, Pallas kernels for 0%

profile of v1, /device:TPU:1, one launch (start us, length us, event | category | flops | bytes accessed | tf_op | source)
XLA Modules:
  0.0 1459.0 jit_solution(4785702120035647469)
XLA Ops:
  7.2 0.0 copy-start
  7.2 0.8 compare_select_fusion
  8.0 0.1 copy.18
  8.1 0.1 reshape.145
  8.2 1.1 fusion.12
  9.3 25.3 %all_gather.12 = bf16[1024,128]{1,0:T(8,128)(2,1)S(1)} all-gather(bf16[256,128]{1,0:T(8,128)(2,1)S(1)} %fusion.12), channel_id=1, replica_groups=mesh['wide'=128,'narrow'=4] {'narrow'}, dimensions={0}, use_global_device_ids=true | all-gather | bytes 327680 | tf_op jit(solution)/shard_map/all_gather | solution.py:54
  34.5 0.0 copy-start.8
  34.5 0.0 copy-start.9
  34.5 0.0 copy-start.10
  34.5 0.0 copy-start.11
  34.6 25.7 %gather_fusion = bf16[7168,128]{1,0:T(8,128)(2,1)} fusion(bf16[1024,128]{1,0:T(8,128)(2,1)S(1)} %all_gather.12, s32[7168]{0:T(1024)S(1)} %broadcast_clamp_fusion), kind=kCustom, calls=%fused_computation | custom fusion | bytes 3698688 | tf_op jit(solution)/shard_map/gather | solution.py:55
  60.3 13.1 all-to-all-start
  73.4 0.2 all-gather.3.cloned.1.call-start
  75.0 0.0 copy-done.8
  75.0 0.0 copy-done.9
  75.0 0.1 fusion.17
  75.1 0.0 copy-done.10
  75.1 0.0 copy-done.11
  75.1 44.7 %all-to-all-done = bf16[128,56,128]{2,1,0:T(8,128)(2,1)S(1)} async-done(((bf16[128,56,128]{2,1,0:T(8,128)(2,1)}), bf16[128,56,128]{2,1,0:T(8,128)(2,1)S(1)}, u32[]{:S(2)}, u32[]{:S(2)}) %all-to-all-start) | async-done | bytes 1835040 | tf_op jit(solution)/shard_map/all_to_all | solution.py:56
  119.8 0.0 copy-start.2
  119.8 1.3 copy-done.2
  121.1 1.7 pad_maximum_fusion.3
  122.8 0.0 copy-start.4
  122.8 2.9 gather_fusion.1
  125.7 0.0 copy-done.4
  125.7 4.4 fusion.5
  130.1 0.0 copy-start.3
  130.2 0.0 copy-start.6
  130.2 0.0 copy-start.7
  130.2 7.1 fusion.6
  137.2 0.0 copy-done.3
  137.3 0.0 copy-done.6
  137.3 0.0 copy-done.7
  137.3 0.2 fusion.13
  137.5 18.2 %all_gather.13 = bf16[1024,128]{1,0:T(8,128)(2,1)S(1)} all-gather(bf16[256,128]{1,0:T(8,128)(2,1)S(1)} %fusion.13), channel_id=1, replica_groups=mesh['wide'=128,'narrow'=4] {'narrow'}, dimensions={0}, use_global_device_ids=true | all-gather | bytes 327680 | tf_op jit(solution)/shard_map/all_gather | solution.py:54
  155.7 21.1 %gather_fusion.2 = bf16[7168,128]{1,0:T(8,128)(2,1)S(1)} fusion(bf16[1024,128]{1,0:T(8,128)(2,1)S(1)} %all_gather.13, s32[7168]{0:T(1024)S(1)} %broadcast_clamp_fusion), kind=kCustom, calls=%fused_computation.2 | custom fusion | bytes 3698688 | tf_op jit(solution)/shard_map/gather | solution.py:55
  176.8 53.5 %all_to_all.10 = bf16[128,56,128]{2,1,0:T(8,128)(2,1)S(1)} all-to-all(bf16[128,56,128]{2,1,0:T(8,128)(2,1)S(1)} %bitcast.54), channel_id=1, replica_groups=mesh['wide'=128,'narrow'=4] {'wide'}, dimensions={0} | all-to-all | bytes 3670016 | tf_op jit(solution)/shard_map/all_to_all | solution.py:56
  230.3 0.2 pad_maximum_fusion.4
  230.5 2.9 gather_fusion.3
  233.4 4.4 fusion.4
  237.8 7.1 fusion.9
  244.9 0.0 copy-done
  245.0 0.0 copy-start.5
  245.0 0.8 convolution_bitcast_fusion
  245.8 0.0 all-gather.3.cloned.1.call-update
  245.8 1184.4 %all-gather.3.cloned.1.call-done = f32[65536,128]{0,1:T(8,128)} async-done(((f32[128,128]{0,1:T(8,128)}), f32[65536,128]{0,1:T(8,128)}) %all-gather.3.cloned.1.call-update) | async-done | bytes 33554448 | tf_op jit(solution)/shard_map/all_gather | solution.py:68
  1430.2 17.2 %copy.24 = f32[16,8,512,128]{3,2,1,0:T(8,128)S(1)} copy(f32[16,8,512,128]{3,1,2,0:T(8,128)} %bitcast.48) | data formatting | bytes 67108864
  1447.4 0.0 copy-done.5
  1447.4 0.0 copy-start.1
  1447.4 4.0 bitcast_reduce_fusion
  1451.4 0.7 copy.23
  1452.2 0.0 copy-done.1
  (12 shorter events, 0.1 us)
Async XLA Ops:
  7.2 237.8 %copy-start = (bf16[256,128]{1,0:T(8,128)(2,1)S(1)}, bf16[256,128]{1,0:T(8,128)(2,1)}, u32[]{:S(2)}) copy-start(bf16[256,128]{1,0:T(8,128)(2,1)} %param.15) | copy-start | bytes 196612
  34.5 40.4 %copy-start.8 = (s32[1,112]{1,0:T(1,128)S(1)}, s32[1,112]{1,0:T(1,128)}, u32[]{:S(2)}) copy-start(s32[1,112]{1,0:T(1,128)} %param.23) | copy-start | bytes 1348
  34.5 40.4 %copy-start.9 = (s32[1,8]{1,0:T(1,128)S(1)}, s32[1,8]{1,0:T(1,128)}, u32[]{:S(2)}) copy-start(s32[1,8]{1,0:T(1,128)} %param.19) | copy-start | bytes 100
  34.5 40.5 %copy-start.10 = (s32[1,112]{1,0:T(1,128)S(1)}, s32[1,112]{1,0:T(1,128)}, u32[]{:S(2)}) copy-start(s32[1,112]{1,0:T(1,128)} %param.22) | copy-start | bytes 1348
  34.5 40.6 %copy-start.11 = (s32[1,8]{1,0:T(1,128)S(1)}, s32[1,8]{1,0:T(1,128)}, u32[]{:S(2)}) copy-start(s32[1,8]{1,0:T(1,128)} %param.18) | copy-start | bytes 100
  60.3 59.5 %all-to-all-start = ((bf16[128,56,128]{2,1,0:T(8,128)(2,1)}), bf16[128,56,128]{2,1,0:T(8,128)(2,1)S(1)}, u32[]{:S(2)}, u32[]{:S(2)}) async-start(bf16[128,56,128]{2,1,0:T(8,128)(2,1)} %bitcast.53), calls=%async_computation | async-start | bytes 3670016 | tf_op jit(solution)/shard_map/all_to_all | solution.py:56
  73.4 1356.8 %all-gather.3.cloned.1.call-start = ((), (), s32[]{:S(2)}) async-start(), calls=%async_computation.2 | async-start | bytes 33619968 | tf_op jit(solution)/shard_map/all_gather | solution.py:68
  119.8 1.3 copy-start.2
  122.8 2.9 copy-start.4
  130.1 7.1 copy-start.3
  130.2 7.1 copy-start.6
  130.2 7.1 copy-start.7
  245.0 1202.5 %copy-start.5 = (f32[256,128]{1,0:T(8,128)}, f32[256,128]{1,0:T(8,128)S(1)}, u32[]{:S(2)}) copy-start(f32[256,128]{1,0:T(8,128)S(1)} %bitcast_add_fusion) | copy-start | bytes 393220
  1447.4 4.7 copy-start.1
Sparse Core Ops, SparseCore 0:
  245.9 1184.2 all-gather.2
